TPU v7x, 32 devices: a whole 2x2x4 slice. The times are simulated.
32 devices in a mesh: scan: 8 (over y, x, core), tile: 4 (over z).
Axes of the slice: x: 2, y: 2, z: 4, core: 2. Of those that a mesh axis runs over, the one named last changes fastest.
Arguments:
- pointing: bfloat16 [8, 2048, 2048], P('tile', 'scan'), may hold values from -0.125 to 0.125
- ground_bin: int32 [8, 2048], P('tile', 'scan'), may hold values from 0 to 23
- degrees: int32 [8], P('tile'), may hold values from 2 to 8
- lengths: int32 [8], P('tile'), may hold values from 1 to 2048, 10240 in all
- tile_lists: int32 [8, 16], P('tile'), may hold values from 0 to 31, as said below
- owner_map: int32 [32], replicated, may hold values from 0 to 3, as said below
Outputs:
- obs_matrix: float32 [4096, 4096], P('tile', 'scan')
Inputs may be any that keep to these rules, and one draw needn't show every extreme that they name: `owner_map`: for each j < 8, entries j * 4 to (j + 1) * 4 - 1 hold every owner 0 to 3 once. `tile_lists`: in each row, entries j * 2 to (j + 1) * 2 - 1 are distinct tiles of j * 4 to (j + 1) * 4 - 1; over the 2 rows of one index of tile, every owner is named (through owner_map) by exactly 8 entries.
All inputs are finite; a program needn't handle non-finite values. No bound on the sum of `lengths` on one device may be relied on, other than what follows from the above.
Results may differ from a plain program's by a relative error of at most 0.0003.
Values may be sent and summed in bfloat16 or wider, within the bound.
A program may use at most 128 MiB of HBM per device.

v0:
```python
import jax
import jax.numpy as jnp
from jax import lax
from jax.sharding import PartitionSpec as P

DEG_MAX = 8
NGB = 24


def build_templates(ground_rows, lengths, degrees):
    sample_rows = ground_rows.shape[1]
    position = jnp.arange(sample_rows).astype(jnp.float32)
    length_value = lengths.astype(jnp.float32)[:, None]
    inside = position[None, :] < length_value
    coord = 2.0 * (position[None, :] + 0.5) / length_value - 1.0
    columns = []
    previous = jnp.ones_like(coord)
    current = coord
    for degree in range(1, DEG_MAX + 1):
        keep = jnp.logical_and(inside, (degree <= degrees)[:, None])
        columns.append(jnp.where(keep, current, jnp.float32(0.0)))
        following = ((2.0 * degree + 1.0) * coord * current - degree * previous) / (degree + 1.0)
        previous, current = (current, following)
    poly_part = jnp.stack(columns, axis=2)
    bins = jnp.logical_and(
        ground_rows[:, :, None] == jnp.arange(NGB)[None, None, :], inside[:, :, None]
    ).astype(jnp.float32)
    return jnp.concatenate([poly_part, bins], axis=2).astype(jnp.bfloat16)


def per_device(pointing, ground_bin, degrees, lengths, tile_lists, owner_map):
    scan_count, sample_rows, width = pointing.shape
    n_scan = lax.axis_size("scan")
    n_tile = lax.axis_size("tile")
    scan_index = lax.axis_index("scan")
    k_tiles = tile_lists.shape[1]
    k_cols = k_tiles // n_scan
    tile_pixels = width // k_tiles
    col_width = k_cols * tile_pixels
    template_cols = DEG_MAX + NGB
    first_local = scan_index * sample_rows
    position = first_local + jnp.arange(sample_rows)
    inside = position[None, :] < lengths[:, None]
    masked = jnp.where(inside[:, :, None], pointing, jnp.zeros_like(pointing))
    first_col = scan_index * col_width
    point_rows = lax.all_gather(masked, "scan", axis=1, tiled=True)
    ground_rows = lax.all_gather(ground_bin, "scan", axis=1, tiled=True)
    template = build_templates(ground_rows, lengths, degrees)
    own_cols = lax.dynamic_slice_in_dim(point_rows, first_col, col_width, 2)
    gram_part = jnp.einsum("snp,snq->spq", point_rows, own_cols, preferred_element_type=jnp.float32)
    proj_part = jnp.einsum("snt,snp->stp", template, point_rows, preferred_element_type=jnp.float32)
    norm_part = jnp.einsum("snt,snu->stu", template, template, preferred_element_type=jnp.float32)
    normal = norm_part + jnp.eye(template_cols, dtype=jnp.float32)[None, :, :]
    factor = jnp.linalg.cholesky(normal)
    whitened = jax.scipy.linalg.solve_triangular(factor, proj_part, lower=True)
    whitened_cols = lax.dynamic_slice_in_dim(whitened, first_col, col_width, 2)
    correction = jnp.einsum(
        "stp,stq->spq", whitened, whitened_cols, precision=lax.Precision.HIGHEST
    )
    contrib = gram_part - correction
    tile_rows = contrib.reshape(scan_count * k_tiles, tile_pixels, col_width)
    row_tiles = tile_lists.reshape(-1)
    matches = row_tiles[:, None] == jnp.arange(owner_map.shape[0])[None, :]
    owners = jnp.sum(jnp.where(matches, owner_map[None, :], 0), axis=1)
    row_total = scan_count * k_tiles
    capacity = row_total // n_tile
    ordering = jnp.argsort(owners * row_total + jnp.arange(row_total), stable=True)
    local_cols = (
        lax.dynamic_slice_in_dim(tile_lists, scan_index * k_cols, k_cols, 1) - scan_index * n_tile
    )
    local_cols = jnp.repeat(local_cols, k_tiles, axis=0)
    labels = jnp.concatenate([(row_tiles // n_tile)[:, None], local_cols], axis=1)
    send_rows = tile_rows[ordering].reshape(n_tile, capacity, tile_pixels, col_width)
    send_labels = labels[ordering].reshape(n_tile, capacity, 1 + k_cols)
    recv_rows, recv_labels = (
        lax.all_to_all(send_rows, "tile", split_axis=0, concat_axis=0, tiled=True),
        lax.all_to_all(send_labels, "tile", split_axis=0, concat_axis=0, tiled=True),
    )
    item_total = n_tile * capacity
    recv_rows = recv_rows.reshape(item_total, tile_pixels, k_cols, tile_pixels)
    recv_labels = recv_labels.reshape(item_total, 1 + k_cols)
    row_select = (recv_labels[:, 0:1] == jnp.arange(n_scan)[None, :]).astype(jnp.float32)
    col_select = (recv_labels[:, 1:, None] == jnp.arange(n_tile)[None, None, :]).astype(jnp.float32)
    placing = row_select[:, :, None, None] * col_select[:, None, :, :]
    placed = jnp.einsum("irkc,ixky->rxcy", placing, recv_rows, precision=lax.Precision.HIGHEST)
    return placed.reshape(n_scan * tile_pixels, n_tile * tile_pixels)


def solution(mesh):
    return jax.shard_map(
        per_device,
        mesh=mesh,
        in_specs=(
            P("tile", "scan", None),
            P("tile", "scan"),
            P("tile"),
            P("tile"),
            P("tile", None),
            P(),
        ),
        out_specs=P("tile", "scan"),
        check_vma=False,
    )
```

profile of v0, /device:TPU:0, one launch (start us, length us, event | category | flops | bytes accessed | tf_op | source)
XLA Modules:
  0.0 256.5 jit_solution(18068372328089807770)
XLA Ops:
  6.6 0.7 broadcast_compare_fusion.1
  7.3 3.1 %broadcast_select_fusion = bf16[2,256,2048]{2,1,0:T(8,128)(2,1)} fusion(bf16[2,256,2048]{2,1,0:T(8,128)(2,1)} %param.6, pred[2,256]{1,0:T(4,128)(4,1)S(1)} %broadcast_compare_fusion.1), kind=kLoop, calls=%fused_computation.6 | loop fusion | flops 1048576 | bytes 4194816 | tf_op jit(solution)/shard_map/jit(_where)/select_n | solution.py:44
  10.7 0.1 copy.47
  10.9 0.1 reshape.1176
  11.0 0.1 copy.48
  11.1 0.2 select_reduce_fusion.1
  11.3 1.6 sort.17
  12.9 0.6 gather_fusion.1
  13.5 0.7 copy.50
  14.2 6.3 %all-to-all-start.1 = ((s32[4,8,3]{1,2,0:T(4,128)}), s32[4,8,3]{1,2,0:T(4,128)S(1)}, u32[]{:S(2)}, u32[]{:S(2)}) async-start(s32[4,8,3]{1,2,0:T(4,128)} %copy.50), calls=%async_computation.1 | async-start | bytes 16384 | tf_op jit(solution)/shard_map/all_to_all | solution.py:77
  20.5 8.9 %all_gather.7 = s32[2,2048]{1,0:T(2,128)S(1)} all-gather(s32[2,256]{1,0:T(2,128)S(1)} %copy-done), channel_id=1, replica_groups=mesh['scan'=8,'tile'=4] {'scan'}, dimensions={1}, use_global_device_ids=true | all-gather | bytes 18432 | tf_op jit(solution)/shard_map/all_gather | solution.py:47
  29.5 0.4 fusion.29
  30.0 0.3 concatenate.7
  30.3 0.2 fusion.34
  30.5 0.1 copy.44
  30.6 5.9 %custom-call.8 = f32[2,32,32]{2,1,0:T(8,128)S(1)} custom-call(f32[2,32,32]{2,1,0:T(8,128)S(1)} %fusion.16), custom_call_target="Cholesky" | custom-call | tf_op jit(solution)/shard_map/jit(cholesky)/cholesky | solution.py:54
  36.5 0.1 compare_reduce_fusion
  36.7 4.9 %custom-call.9 = f32[2,1,32,32]{2,3,1,0:T(8,128)S(1)} custom-call(f32[2,1,32,32]{3,2,1,0:T(8,128)S(1)} %select_bitcast_fusion), custom_call_target="InvertDiagBlocksLowerTriangular" | custom-call | tf_op jit(solution)/shard_map/jit(_solve_triangular)/vmap()/triangular_solve | solution.py:55
  41.6 61.6 %all-gather.2.cloned.1.call-done = bf16[2,2048,2048]{2,1,0:T(8,128)(2,1)} async-done(((bf16[2,256,2048]{2,1,0:T(8,128)(2,1)}), bf16[2,2048,2048]{2,1,0:T(8,128)(2,1)}) %all-gather.2.cloned.1.call-update) | async-done | bytes 16777232 | tf_op jit(solution)/shard_map/all_gather | solution.py:46
  103.3 8.7 %fusion.35 = f32[2,32,2048]{2,1,0:T(8,128)S(1)} fusion(bf16[2,2048,32]{1,2,0:T(8,128)(2,1)S(1)} %concatenate.7, bf16[2,2048,2048]{2,1,0:T(8,128)(2,1)} %all-gather.2.cloned.1.call-done), kind=kOutput, calls=%fused_computation.92 | convolution fusion | flops 536870912 | bytes 17563648 | tf_op jit(solution)/shard_map/snt,snp->stp/dot_general | solution.py:51
  112.0 0.6 fusion.13
  112.7 10.7 %fusion = f32[2,2048,256]{2,1,0:T(8,128)S(1)} fusion(bf16[2,2048,2048]{2,1,0:T(8,128)(2,1)} %all-gather.2.cloned.1.call-done, s32[]{:T(128)S(6)} %select_n.117), kind=kOutput, calls=%fused_computation.4 | convolution fusion | flops 4294967296 | bytes 23068676 | tf_op jit(solution)/shard_map/snp,snq->spq/dot_general | solution.py:50
  123.4 5.0 %convolution_subtract_fusion = f32[2,2048,256]{2,1,0:T(8,128)} fusion(f32[2,2048,256]{2,1,0:T(8,128)S(1)} %fusion, f32[2,32,2048]{2,1,0:T(8,128)S(1)} %fusion.13, s32[]{:T(128)S(6)} %select_n.117), kind=kOutput, calls=%fused_computation.2 | convolution fusion | flops 403701760 | bytes 8978436 | tf_op jit(solution)/shard_map/stp,stq->spq/dot_general | solution.py:57
  128.4 5.0 %gather_fusion = f32[32,128,256]{2,1,0:T(8,128)} fusion(f32[32,128,256]{2,1,0:T(8,128)} %bitcast.45, s32[1024]{0:T(1024)S(1)} %pad_clamp_fusion), kind=kCustom, calls=%fused_computation | custom fusion | bytes 8388736 | tf_op jit(solution)/shard_map/gather | solution.py:73
  133.4 5.6 %copy.46 = f32[32,128,256]{1,2,0:T(8,128)} copy(f32[32,128,256]{2,1,0:T(8,128)} %gather_fusion) | data formatting | bytes 8388608 | tf_op jit(solution)/shard_map/gather | solution.py:73
  139.0 5.0 %all-to-all-start = ((f32[4,8,128,256]{2,3,1,0:T(8,128)}), f32[4,8,128,256]{2,3,1,0:T(8,128)}, u32[]{:S(2)}, u32[]{:S(2)}) async-start(f32[4,8,128,256]{2,3,1,0:T(8,128)} %bitcast.44), calls=%async_computation | async-start | bytes 8388608 | tf_op jit(solution)/shard_map/all_to_all | solution.py:76
  144.0 0.1 reshape.1178
  144.1 93.6 %all-to-all-done = f32[4,8,128,256]{2,3,1,0:T(8,128)} async-done(((f32[4,8,128,256]{2,3,1,0:T(8,128)}), f32[4,8,128,256]{2,3,1,0:T(8,128)}, u32[]{:S(2)}, u32[]{:S(2)}) %all-to-all-start) | async-done | bytes 4194336 | tf_op jit(solution)/shard_map/all_to_all | solution.py:76
  237.7 5.5 %copy.57 = f32[32,128,2,128,1]{3,0,2,4,1:T(8,128)} copy(f32[32,128,2,128,1]{1,3,2,0,4:T(8,128)} %bitcast.6) | data formatting | bytes 8388608 | tf_op jit(solution)/shard_map/reshape | solution.py:80
  243.2 4.3 %convolution_bitcast_fusion = f32[8,128,4,128]{3,0,2,1:T(8,128)S(1)} fusion(f32[32,128,2,128,1]{3,0,2,4,1:T(8,128)} %copy.57, f32[32,2,4]{0,1,2:T(2,128)S(1)} %compare_convert_fusion, f32[32,8]{0,1:T(8,128)S(1)} %fusion.31), kind=kOutput, calls=%fused_computation.7 | convolution fusion | flops 402655232 | bytes 6293504 | tf_op jit(solution)/shard_map/irkc,ixky->rxcy/dot_general | solution.py:85
  247.6 0.5 copy.63
  248.1 1.5 copy.67
  (41 shorter events, 0.8 us)
Async XLA Ops:
  6.5 14.0 %copy-start.2 = (s32[2]{0:T(128)S(1)}, s32[2]{0:T(128)}, u32[]{:S(2)}) copy-start(s32[2]{0:T(128)} %param.9) | copy-start | bytes 28
  6.5 3.9 %copy-start.1 = (s32[2,16]{1,0:T(2,128)S(1)}, s32[2,16]{1,0:T(2,128)}, u32[]{:S(2)}) copy-start(s32[2,16]{1,0:T(2,128)} %param.10) | copy-start | bytes 388
  6.5 4.6 %copy-start.4 = (s32[32]{0:T(128)S(1)}, s32[32]{0:T(128)}, u32[]{:S(2)}) copy-start(s32[32]{0:T(128)} %param.11) | copy-start | bytes 388
  6.5 14.0 %copy-start = (s32[2,256]{1,0:T(2,128)S(1)}, s32[2,256]{1,0:T(2,128)}, u32[]{:S(2)}) copy-start(s32[2,256]{1,0:T(2,128)} %param.7) | copy-start | bytes 6148
  6.5 22.9 %copy-start.3 = (s32[2]{0:T(128)S(1)}, s32[2]{0:T(128)}, u32[]{:S(2)}) copy-start(s32[2]{0:T(128)} %param.8) | copy-start | bytes 28
  6.5 96.7 %all-gather.2.cloned.1.call-start = ((), (), s32[]{:S(2)}) async-start(), calls=%async_computation.2 | async-start | bytes 18874368 | tf_op jit(solution)/shard_map/all_gather | solution.py:46
  14.2 124.8 %all-to-all-start.1 = ((s32[4,8,3]{1,2,0:T(4,128)}), s32[4,8,3]{1,2,0:T(4,128)S(1)}, u32[]{:S(2)}, u32[]{:S(2)}) async-start(s32[4,8,3]{1,2,0:T(4,128)} %copy.50), calls=%async_computation.1 | async-start | bytes 16384 | tf_op jit(solution)/shard_map/all_to_all | solution.py:77
  139.0 98.8 %all-to-all-start = ((f32[4,8,128,256]{2,3,1,0:T(8,128)}), f32[4,8,128,256]{2,3,1,0:T(8,128)}, u32[]{:S(2)}, u32[]{:S(2)}) async-start(f32[4,8,128,256]{2,3,1,0:T(8,128)} %bitcast.44), calls=%async_computation | async-start | bytes 8388608 | tf_op jit(solution)/shard_map/all_to_all | solution.py:76
Sparse Core Ops, SparseCore 0:
  10.6 92.6 all-gather.1
where the time goes:
time: 257 us; the launch traced here: 256 us
  waiting for transfers between devices  155 us (60%)
  matrix products  29.7 us (12%)
  local copies, waits for them, and re-layouts  20.3 us (8%)
  other arithmetic  17.4 us (7%)
  between operations  13.6 us (5%)
  starting transfers between devices  11.4 us (4%)
  blocking collectives  8.92 us (3%)
    all_to_all x1, waiting for transfers between devices, per_device(): lax.all_to_all(send_rows, 'tile', split_axis=0, concat_axis=0, tiled=True)  93.6 us
    all_gather x1, waiting for transfers between devices, per_device(): point_rows = lax.all_gather(masked, 'scan', axis=1, tiled=True)  61.6 us
    dot_general x1, matrix products, per_device(): jnp.einsum('snp,snq->spq', point_rows, own_cols, preferred_element_type=j...  10.7 us
    gather x2, local copies, waits for them, and re-layouts, per_device(): tile_rows[ordering].reshape(n_tile, capacity, tile_pixels, col_width)  10.5 us
    all_gather x1, blocking collectives, per_device(): ground_rows = lax.all_gather(ground_bin, 'scan', axis=1, tiled=True)  8.92 us
    dot_general x1, matrix products, per_device(): jnp.einsum('snt,snp->stp', template, point_rows, preferred_element_type=j...  8.75 us
    all_to_all x1, starting transfers between devices, per_device(): lax.all_to_all(send_labels, 'tile', split_axis=0, concat_axis=0, tiled=True)  6.32 us
    another operation x4, other arithmetic, per_device(): factor = jnp.linalg.cholesky(normal)  6.03 us
  transfers between devices with their start and end apart: 3, of which 2 were waited for; matrix products, arithmetic and copies ran while one was open for 20% of the time, Pallas kernels for 0%

commit v1 on v0

v1 whole, which is shorter than its diff:
```python
import functools

import jax
import jax.numpy as jnp
from jax import lax
from jax.experimental import pallas as pl
from jax.experimental.pallas import tpu as pltpu
from jax.sharding import PartitionSpec as P

DEG_MAX = 8
NGB = 24
STEPS = 32.0
LIMIT = 32000.0
HIGH = lax.Precision.HIGHEST


def build_templates_t(ground_rows, lengths, degrees):
    sample_rows = ground_rows.shape[1]
    position = jnp.arange(sample_rows).astype(jnp.float32)
    length_value = lengths.astype(jnp.float32)[:, None]
    inside = position[None, :] < length_value
    coord = 2.0 * (position[None, :] + 0.5) / length_value - 1.0
    columns = []
    previous = jnp.ones_like(coord)
    current = coord
    for degree in range(1, DEG_MAX + 1):
        keep = jnp.logical_and(inside, (degree <= degrees)[:, None])
        columns.append(jnp.where(keep, current, jnp.float32(0.0)))
        following = ((2.0 * degree + 1.0) * coord * current - degree * previous) / (degree + 1.0)
        previous, current = (current, following)
    poly_part = jnp.stack(columns, axis=1)
    bins = jnp.logical_and(
        ground_rows[:, None, :] == jnp.arange(NGB)[None, :, None], inside[:, None, :]
    ).astype(jnp.float32)
    return jnp.concatenate([poly_part, bins], axis=1).astype(jnp.bfloat16)


def contrib_kernel(
    tile_pixels, k_cols, capacity, n_tile,
    order_ref, lengths_ref, place_ref,
    point_ref, own_ref, template_ref, linv_ref, out_ref, own_t, white_own, blocks, scales,
):
    scan, chunk = pl.program_id(0), pl.program_id(1)
    scan_count, chunk_count = pl.num_programs(0), pl.num_programs(1)
    samples, col_width = own_ref.shape[1:]
    chunk_width = point_ref.shape[2]
    per_chunk = chunk_width // tile_pixels
    contract_last = (((1,), (1,)), ((), ()))

    @pl.when(chunk == 0)
    def _():
        position = lax.broadcasted_iota(jnp.int32, (col_width, samples), 1)
        turned = own_ref[0].T
        own_t[...] = jnp.where(position < lengths_ref[scan], turned, jnp.zeros_like(turned))
        proj = lax.dot_general(
            own_t[...], template_ref[0], contract_last, preferred_element_type=jnp.float32
        )
        white_own[...] = lax.dot_general(
            proj, linv_ref[0], contract_last, precision=HIGH, preferred_element_type=jnp.float32
        )

    gram = jnp.dot(own_t[...], point_ref[0], preferred_element_type=jnp.float32)
    proj = jnp.dot(template_ref[0], point_ref[0], preferred_element_type=jnp.float32)
    white = jnp.dot(linv_ref[0], proj, precision=HIGH, preferred_element_type=jnp.float32)
    total = gram - jnp.dot(
        white_own[...], white, precision=HIGH, preferred_element_type=jnp.float32
    )
    first = (scan * chunk_count + chunk) * per_chunk
    for b in range(per_chunk):
        blocks[first + b] = total[:, b * tile_pixels : (b + 1) * tile_pixels]

    @pl.when(jnp.logical_and(scan == scan_count - 1, chunk == chunk_count - 1))
    def _():
        scales[...] = jnp.zeros_like(scales)
        for dest in range(n_tile):

            def one(item, carry):
                entry = order_ref[dest * capacity + item]
                for k in range(k_cols):
                    part = blocks[entry, k * tile_pixels : (k + 1) * tile_pixels, :]
                    top = jnp.max(jnp.abs(part), axis=0, keepdims=True)
                    level = jnp.ceil(jnp.log2(jnp.maximum(top, 1e-30) / LIMIT) * STEPS)
                    coded = jnp.round(part * jnp.exp2(level * (-1.0 / STEPS))).astype(jnp.int32)
                    row = pl.multiple_of((item * k_cols + k) * tile_pixels, tile_pixels)
                    out_ref[dest, pl.ds(row, tile_pixels), :] = coded.astype(jnp.int16)
                    scales[dest, pl.ds(item * k_cols + k, 1), :] = level
                return carry

            lax.fori_loop(0, capacity, one, 0)
            base = capacity * col_width
            out_ref[dest, base:, :] = scales[dest].astype(jnp.int32).astype(jnp.int16)


def place_kernel(
    tile_pixels, group, n_tile, scan_count, index_ref, recv_ref, out_ref, scales
):
    row = pl.program_id(0)
    base = group * tile_pixels

    @pl.when(row == 0)
    def _():
        for source in range(n_tile):
            level = recv_ref[source, base:, :].astype(jnp.float32)
            scales[source] = jnp.exp2(level * (1.0 / STEPS))

    for col in range(n_tile):
        total = jnp.zeros((tile_pixels, tile_pixels), jnp.float32)
        for source in range(n_tile):
            for scan in range(scan_count):
                found = index_ref[((row * n_tile + col) * n_tile + source) * scan_count + scan]
                slot = jnp.maximum(found, 0)
                start = pl.multiple_of(slot * tile_pixels, tile_pixels)
                part = recv_ref[source, pl.ds(start, tile_pixels), :].astype(jnp.float32)
                scale = scales[source, pl.ds(slot, 1), :] * (found >= 0).astype(jnp.float32)
                total = total + part * scale
        out_ref[:, col * tile_pixels : (col + 1) * tile_pixels] = total.T


def per_device(pointing, ground_bin, degrees, lengths, tile_lists, owner_map):
    scan_count, sample_rows, width = pointing.shape
    n_scan = lax.axis_size("scan")
    n_tile = lax.axis_size("tile")
    scan_index = lax.axis_index("scan")
    tile_index = lax.axis_index("tile")
    k_tiles = tile_lists.shape[1]
    k_cols = k_tiles // n_scan
    tile_pixels = width // k_tiles
    col_width = k_cols * tile_pixels
    template_cols = DEG_MAX + NGB
    samples = sample_rows * n_scan
    row_total = scan_count * k_tiles
    capacity = row_total // n_tile
    group = capacity * k_cols
    group_pad = -(-group // 16) * 16

    point_rows = lax.all_gather(pointing, "scan", axis=1, tiled=True)

    small = jnp.concatenate([ground_bin, tile_lists], axis=1)
    small = lax.all_gather(small, ("tile", "scan"), axis=0, tiled=False)
    small = small.reshape(n_tile, n_scan, scan_count, sample_rows + k_tiles)
    ground_rows = lax.dynamic_index_in_dim(small, tile_index, 0, keepdims=False)[:, :, :sample_rows]
    ground_rows = ground_rows.transpose(1, 0, 2).reshape(scan_count, samples)
    all_lists = small[:, 0, :, sample_rows:]

    template = build_templates_t(ground_rows, lengths, degrees)
    normal = jnp.einsum("stn,sun->stu", template, template, preferred_element_type=jnp.float32)
    normal = normal + jnp.eye(template_cols, dtype=jnp.float32)[None, :, :]
    factor = jnp.linalg.cholesky(normal)
    eye = jnp.broadcast_to(jnp.eye(template_cols, dtype=jnp.float32)[None], normal.shape)
    linv = jax.scipy.linalg.solve_triangular(factor, eye, lower=True)

    tiles = jnp.arange(owner_map.shape[0])
    owners_all = jnp.sum(
        jnp.where(all_lists[..., None] == tiles, owner_map, 0), axis=-1
    ).reshape(n_tile, row_total)
    before = jnp.arange(row_total)[:, None] > jnp.arange(row_total)[None, :]
    same = owners_all[:, :, None] == owners_all[:, None, :]
    rank = jnp.sum(jnp.logical_and(same, before[None]), axis=2)
    my_slot = lax.dynamic_index_in_dim(owners_all * capacity + rank, tile_index, 0, keepdims=False)
    order = jnp.sum(
        jnp.where(my_slot[None, :] == jnp.arange(row_total)[:, None], jnp.arange(row_total)[None, :], 0),
        axis=1,
    ).astype(jnp.int32)

    mine = (owners_all == tile_index).reshape(n_tile, scan_count, k_tiles)
    rank = rank.reshape(n_tile, scan_count, k_tiles)
    row_hit = jnp.logical_and(
        mine[None], (all_lists // n_tile)[None] == jnp.arange(n_scan)[:, None, None, None]
    )
    row_item = jnp.sum(jnp.where(row_hit, rank[None] + 1, 0), axis=-1)
    my_cols = lax.dynamic_slice_in_dim(all_lists, scan_index * k_cols, k_cols, 2) - scan_index * n_tile
    col_hit = my_cols[None] == jnp.arange(n_tile)[:, None, None, None]
    col_item = jnp.sum(jnp.where(col_hit, jnp.arange(k_cols) + 1, 0), axis=-1)
    found = jnp.where(
        jnp.logical_and(row_item[:, None] > 0, col_item[None] > 0),
        (row_item[:, None] - 1) * k_cols + col_item[None] - 1,
        -1,
    )
    index = found.reshape(-1).astype(jnp.int32)

    chunk_width = min(4 * tile_pixels, width)
    send = pl.pallas_call(
        functools.partial(contrib_kernel, tile_pixels, k_cols, capacity, n_tile),
        grid_spec=pltpu.PrefetchScalarGridSpec(
            num_scalar_prefetch=3,
            grid=(scan_count, width // chunk_width),
            in_specs=[
                pl.BlockSpec((1, samples, chunk_width), lambda s, c, o, l, j: (s, 0, c)),
                pl.BlockSpec((1, samples, col_width), lambda s, c, o, l, j: (s, 0, j[0])),
                pl.BlockSpec((1, template_cols, samples), lambda s, c, o, l, j: (s, 0, 0)),
                pl.BlockSpec((1, template_cols, template_cols), lambda s, c, o, l, j: (s, 0, 0)),
            ],
            out_specs=pl.BlockSpec(
                (n_tile, group * tile_pixels + group_pad, tile_pixels), lambda s, c, o, l, j: (0, 0, 0)
            ),
            scratch_shapes=[
                pltpu.VMEM((col_width, samples), jnp.bfloat16),
                pltpu.VMEM((col_width, template_cols), jnp.float32),
                pltpu.VMEM((row_total, col_width, tile_pixels), jnp.float32),
                pltpu.VMEM((n_tile, group_pad, tile_pixels), jnp.float32),
            ],
        ),
        out_shape=jax.ShapeDtypeStruct(
            (n_tile, group * tile_pixels + group_pad, tile_pixels), jnp.int16
        ),
        compiler_params=pltpu.CompilerParams(vmem_limit_bytes=48 * 1024 * 1024),
    )(order, lengths, scan_index[None].astype(jnp.int32), point_rows, point_rows, template, linv)

    recv = lax.all_to_all(send, "tile", split_axis=0, concat_axis=0, tiled=True)

    return pl.pallas_call(
        functools.partial(place_kernel, tile_pixels, group, n_tile, scan_count),
        grid_spec=pltpu.PrefetchScalarGridSpec(
            num_scalar_prefetch=1,
            grid=(n_scan,),
            in_specs=[pl.BlockSpec(recv.shape, lambda r, i: (0, 0, 0))],
            out_specs=pl.BlockSpec((tile_pixels, n_tile * tile_pixels), lambda r, i: (r, 0)),
            scratch_shapes=[pltpu.VMEM((n_tile, group_pad, tile_pixels), jnp.float32)],
        ),
        out_shape=jax.ShapeDtypeStruct((n_scan * tile_pixels, n_tile * tile_pixels), jnp.float32),
        compiler_params=pltpu.CompilerParams(vmem_limit_bytes=32 * 1024 * 1024),
    )(index, recv)


def solution(mesh):
    return jax.shard_map(
        per_device,
        mesh=mesh,
        in_specs=(
            P("tile", "scan", None),
            P("tile", "scan"),
            P("tile"),
            P("tile"),
            P("tile", None),
            P(),
        ),
        out_specs=P("tile", "scan"),
        check_vma=False,
    )
```

time: 257 us -> 190 us (0.74)
  waiting for transfers between devices: 155 us -> 85.2 us
  blocking collectives: 8.92 us -> 44.1 us
  matrix products: 29.7 us -> 0.44 us
  Pallas kernels: 0 us -> 26.6 us
  local copies, waits for them, and re-layouts: 20.3 us -> 1.39 us
  starting transfers between devices: 11.4 us -> 4.72 us
  other arithmetic: 17.4 us -> 13.3 us
    all_to_all x2 -> x1, waiting for transfers between devices: 93.6 us -> 47.8 us  [per_device(): recv = lax.all_to_all(send, 'tile', split_axis=0, concat_axis=0, tiled=True)]
    all_gather x1, blocking collectives: 8.92 us -> 44.1 us  [per_device(): small = lax.all_gather(small, ('tile', 'scan'), axis=0, tiled=False)]
    dot_general x5 -> x1, matrix products: 29 us -> 0.2 us  [per_device(): jnp.einsum('stn,sun->stu', template, template, preferred_element_type=jnp...]
    pallas_call x0 -> x2, Pallas kernels: none -> 26.6 us  [the longest x1 21.4 us: per_device(): pl.pallas_call(functools.partial(contrib_kernel, tile_pixels, k_cols, cap...]
    all_gather x1, waiting for transfers between devices: 61.6 us -> 36.8 us  [per_device(): point_rows = lax.all_gather(pointing, 'scan', axis=1, tiled=True)]
    gather x3 -> x0, local copies, waits for them, and re-layouts: 11.1 us -> none  [the longest x2 10.5 us: per_device(): tile_rows[ordering].reshape(n_tile, capacity, tile_pixels, col_width)]
    reshape x6 -> x0, local copies, waits for them, and re-layouts: 6.99 us -> none  [the longest x1 5.51 us: per_device(): recv_rows = recv_rows.reshape(item_total, tile_pixels, k_cols, tile_pixels)]
    all_to_all x2 -> x1, starting transfers between devices: 11.3 us -> 4.69 us  [per_device(): recv = lax.all_to_all(send, 'tile', split_axis=0, concat_axis=0, tiled=True)]
  transfers between devices with their start and end apart: 3 -> 2, of which waited for: 2 -> 2; matrix products, arithmetic and copies ran while one was open for 20% -> 8% of each run, Pallas kernels for 0% -> 0%
where the time goes in v1:
time: 190 us; the launch traced here: 189 us
  waiting for transfers between devices  85.2 us (45%)
  blocking collectives  44.1 us (23%)
  Pallas kernels  26.6 us (14%)
  between operations  13.6 us (7%)
  other arithmetic  13.3 us (7%)
  starting transfers between devices  4.72 us (2%)
    all_to_all x1, waiting for transfers between devices, per_device(): recv = lax.all_to_all(send, 'tile', split_axis=0, concat_axis=0, tiled=True)  47.8 us
    all_gather x1, blocking collectives, per_device(): small = lax.all_gather(small, ('tile', 'scan'), axis=0, tiled=False)  44.1 us
    all_gather x1, waiting for transfers between devices, per_device(): point_rows = lax.all_gather(pointing, 'scan', axis=1, tiled=True)  36.8 us
    pallas_call x1, Pallas kernels, per_device(): pl.pallas_call(functools.partial(contrib_kernel, tile_pixels, k_cols, cap...  21.4 us
    another operation x4, other arithmetic, per_device(): factor = jnp.linalg.cholesky(normal)  6.03 us
    pallas_call x1, Pallas kernels, per_device(): pl.pallas_call(functools.partial(place_kernel, tile_pixels, group, n_tile...  5.2 us
    another operation x3, other arithmetic, per_device(): linv = jax.scipy.linalg.solve_triangular(factor, eye, lower=True)  4.99 us
    all_to_all x1, starting transfers between devices, per_device(): recv = lax.all_to_all(send, 'tile', split_axis=0, concat_axis=0, tiled=True)  4.69 us
  transfers between devices with their start and end apart: 2, of which 2 were waited for; matrix products, arithmetic and copies ran while one was open for 8% of the time, Pallas kernels for 0%

profile of v1, /device:TPU:0, one launch (start us, length us, event | category | flops | bytes accessed | tf_op | source)
XLA Modules:
  0.0 189.4 jit_solution(836209797509211897)
XLA Ops:
  6.6 0.7 all-gather.4.cloned.1.call-update
  7.3 0.7 convert_element_type.39
  8.0 44.1 %all-gather.1 = s32[32,2,272]{2,1,0:T(2,128)S(1)} all-gather(s32[1,2,272]{2,1,0:T(2,128)S(1)} %add_bitcast_fusion), channel_id=2, replica_groups=mesh['scan'=8,'tile'=4] {'tile','scan'}, dimensions={0}, use_global_device_ids=true | all-gather | bytes 71808 | tf_op jit(solution)/shard_map/all_gather | solution.py:139
  52.2 0.3 select_reduce_fusion
  52.5 0.1 eq.109
  52.6 0.1 broadcast_compare_fusion
  52.7 0.4 fusion.24
  53.1 0.3 concatenate.8.template_ref
  53.4 0.2 fusion.27
  53.6 0.1 copy.45
  53.7 5.9 %custom-call.8 = f32[2,32,32]{2,1,0:T(8,128)S(1)} custom-call(f32[2,32,32]{2,1,0:T(8,128)S(1)} %fusion.12), custom_call_target="Cholesky" | custom-call | tf_op jit(solution)/shard_map/jit(cholesky)/cholesky | solution.py:148
  59.7 0.1 compare_reduce_fusion
  59.8 0.1 select_bitcast_fusion
  59.9 4.9 %custom-call.9 = f32[2,1,32,32]{2,3,1,0:T(8,128)S(1)} custom-call(f32[2,1,32,32]{3,2,1,0:T(8,128)S(1)} %select_bitcast_fusion), custom_call_target="InvertDiagBlocksLowerTriangular" | custom-call | tf_op jit(solution)/shard_map/jit(_solve_triangular)/vmap()/triangular_solve | solution.py:150
  64.8 0.2 convert_reduce_fusion
  65.1 0.1 select_reduce_fusion.3.order_ref
  65.2 0.2 fusion.9.linv_ref
  65.4 36.8 %all-gather.4.cloned.1.call-done.point_ref.own_ref = bf16[2,2048,2048]{2,1,0:T(8,128)(2,1)} async-done(((bf16[2,256,2048]{2,1,0:T(8,128)(2,1)}), bf16[2,2048,2048]{2,1,0:T(8,128)(2,1)}) %all-gather.4.cloned.1.call-update) | async-done | bytes 16777232 | tf_op jit(solution)/shard_map/all_gather | solution.py:136
  102.2 21.4 %shard_map.64 = s16[4,2064,128]{2,1,0:T(8,128)(2,1)} custom-call(s32[32]{0:T(128)S(1)} %select_reduce_fusion.3.order_ref, s32[2]{0:T(128)S(1)} %copy-done, s32[1]{0:T(128)} %bitcast.5.place_ref, bf16[2,2048,2048]{2,1,0:T(8,128)(2,1)} %all-gather.4.cloned.1.call-done.point_ref.own_ref, bf16[2,2048,2048]{2,1,0:T(8,128)(2,1)} %all-gather.4.cloned.1.call-done.point_ref.own_ref, ...), custom_call_target="tpu_custom_call" | custom-call | tf_op jit(solution)/shard_map/pallas_call | solution.py:182
  123.6 4.7 %all-to-all-start = ((s16[4,2064,128]{2,1,0:T(8,128)(2,1)}), s16[4,2064,128]{2,1,0:T(8,128)(2,1)S(1)}, u32[]{:S(2)}, u32[]{:S(2)}) async-start(s16[4,2064,128]{2,1,0:T(8,128)(2,1)} %shard_map.64), calls=%async_computation | async-start | bytes 4227072 | tf_op jit(solution)/shard_map/all_to_all | solution.py:209
  128.3 0.1 constant_dynamic-slice_fusion.1
  128.3 0.1 copy.50
  128.4 0.1 select_reduce_fusion.4
  128.5 0.1 copy.44
  128.6 0.1 copy.41
  128.8 0.1 add.163
  128.9 0.2 select_reduce_fusion.2
  129.1 0.1 copy.40
  129.2 0.1 copy.43
  129.4 0.1 select_n.133.index_ref
  129.5 47.8 %all-to-all-done.recv_ref = s16[4,2064,128]{2,1,0:T(8,128)(2,1)S(1)} async-done(((s16[4,2064,128]{2,1,0:T(8,128)(2,1)}), s16[4,2064,128]{2,1,0:T(8,128)(2,1)S(1)}, u32[]{:S(2)}, u32[]{:S(2)}) %all-to-all-start) | async-done | bytes 2113568 | tf_op jit(solution)/shard_map/all_to_all | solution.py:209
  177.3 5.2 %shard_map.65 = f32[1024,512]{1,0:T(8,128)} custom-call(s32[256]{0:T(256)S(1)} %select_n.133.index_ref, s16[4,2064,128]{2,1,0:T(8,128)(2,1)S(1)} %all-to-all-done.recv_ref), custom_call_target="tpu_custom_call" | custom-call | tf_op jit(solution)/shard_map/pallas_call | solution.py:211
  (39 shorter events, 0.4 us)
Async XLA Ops:
  6.5 95.7 %copy-start = (s32[2]{0:T(128)S(1)}, s32[2]{0:T(128)}, u32[]{:S(2)}) copy-start(s32[2]{0:T(128)} %lengths_ref.1) | copy-start | bytes 28
  6.5 1.4 copy-start.2
  6.5 1.4 copy-start.1
  6.5 45.6 %copy-start.3 = (s32[32]{0:T(128)S(1)}, s32[32]{0:T(128)}, u32[]{:S(2)}) copy-start(s32[32]{0:T(128)} %param.11) | copy-start | bytes 388
  6.5 46.0 %copy-start.4 = (s32[2]{0:T(128)S(1)}, s32[2]{0:T(128)}, u32[]{:S(2)}) copy-start(s32[2]{0:T(128)} %param.8) | copy-start | bytes 28
  6.5 95.7 %all-gather.4.cloned.1.call-start = ((), (), s32[]{:S(2)}) async-start(), calls=%async_computation.1 | async-start | bytes 18874368 | tf_op jit(solution)/shard_map/all_gather | solution.py:136
  123.6 53.7 %all-to-all-start = ((s16[4,2064,128]{2,1,0:T(8,128)(2,1)}), s16[4,2064,128]{2,1,0:T(8,128)(2,1)S(1)}, u32[]{:S(2)}, u32[]{:S(2)}) async-start(s16[4,2064,128]{2,1,0:T(8,128)(2,1)} %shard_map.64), calls=%async_computation | async-start | bytes 4227072 | tf_op jit(solution)/shard_map/all_to_all | solution.py:209
Sparse Core Ops, SparseCore 0:
  9.3 92.8 all-gather.3

commit v2 on v1

--- a/solution.py
+++ b/solution.py
@@ -36,59 +36,56 @@
 
 
 def contrib_kernel(
-    tile_pixels, k_cols, capacity, n_tile,
-    order_ref, lengths_ref, place_ref,
-    point_ref, own_ref, template_ref, linv_ref, out_ref, own_t, white_own, blocks, scales,
+    tile_pixels, lengths_ref, place_ref,
+    point_ref, own_ref, template_ref, linv_ref, blocks_ref, own_t, white_own,
 ):
-    scan, chunk = pl.program_id(0), pl.program_id(1)
-    scan_count, chunk_count = pl.num_programs(0), pl.num_programs(1)
-    samples, col_width = own_ref.shape[1:]
-    chunk_width = point_ref.shape[2]
-    per_chunk = chunk_width // tile_pixels
+    chunk = pl.program_id(0)
+    samples, col_width = own_ref.shape
+    per_chunk = point_ref.shape[1] // tile_pixels
     contract_last = (((1,), (1,)), ((), ()))
 
     @pl.when(chunk == 0)
     def _():
         position = lax.broadcasted_iota(jnp.int32, (col_width, samples), 1)
-        turned = own_ref[0].T
-        own_t[...] = jnp.where(position < lengths_ref[scan], turned, jnp.zeros_like(turned))
+        turned = own_ref[...].T
+        own_t[...] = jnp.where(position < lengths_ref[0], turned, jnp.zeros_like(turned))
         proj = lax.dot_general(
-            own_t[...], template_ref[0], contract_last, preferred_element_type=jnp.float32
+            own_t[...], template_ref[...], contract_last, preferred_element_type=jnp.float32
         )
         white_own[...] = lax.dot_general(
-            proj, linv_ref[0], contract_last, precision=HIGH, preferred_element_type=jnp.float32
+            proj, linv_ref[...], contract_last, precision=HIGH, preferred_element_type=jnp.float32
         )
 
-    gram = jnp.dot(own_t[...], point_ref[0], preferred_element_type=jnp.float32)
-    proj = jnp.dot(template_ref[0], point_ref[0], preferred_element_type=jnp.float32)
-    white = jnp.dot(linv_ref[0], proj, precision=HIGH, preferred_element_type=jnp.float32)
+    gram = jnp.dot(own_t[...], point_ref[...], preferred_element_type=jnp.float32)
+    proj = jnp.dot(template_ref[...], point_ref[...], preferred_element_type=jnp.float32)
+    white = jnp.dot(linv_ref[...], proj, precision=HIGH, preferred_element_type=jnp.float32)
     total = gram - jnp.dot(
         white_own[...], white, precision=HIGH, preferred_element_type=jnp.float32
     )
-    first = (scan * chunk_count + chunk) * per_chunk
     for b in range(per_chunk):
-        blocks[first + b] = total[:, b * tile_pixels : (b + 1) * tile_pixels]
-
-    @pl.when(jnp.logical_and(scan == scan_count - 1, chunk == chunk_count - 1))
-    def _():
-        scales[...] = jnp.zeros_like(scales)
-        for dest in range(n_tile):
-
-            def one(item, carry):
-                entry = order_ref[dest * capacity + item]
-                for k in range(k_cols):
-                    part = blocks[entry, k * tile_pixels : (k + 1) * tile_pixels, :]
-                    top = jnp.max(jnp.abs(part), axis=0, keepdims=True)
-                    level = jnp.ceil(jnp.log2(jnp.maximum(top, 1e-30) / LIMIT) * STEPS)
-                    coded = jnp.round(part * jnp.exp2(level * (-1.0 / STEPS))).astype(jnp.int32)
-                    row = pl.multiple_of((item * k_cols + k) * tile_pixels, tile_pixels)
-                    out_ref[dest, pl.ds(row, tile_pixels), :] = coded.astype(jnp.int16)
-                    scales[dest, pl.ds(item * k_cols + k, 1), :] = level
-                return carry
-
-            lax.fori_loop(0, capacity, one, 0)
-            base = capacity * col_width
-            out_ref[dest, base:, :] = scales[dest].astype(jnp.int32).astype(jnp.int16)
+        blocks_ref[b] = total[:, b * tile_pixels : (b + 1) * tile_pixels]
+
+
+def code_kernel(tile_pixels, k_cols, capacity, order_ref, *refs):
+    *block_refs, out_ref, scales = refs
+    k_tiles, col_width = block_refs[0].shape[:2]
+    dest = pl.program_id(0)
+    scales[...] = jnp.zeros_like(scales)
+    for item in range(capacity):
+        entry = order_ref[dest * capacity + item]
+        scan, place = entry // k_tiles, entry % k_tiles
+        for k in range(k_cols):
+            rows = slice(k * tile_pixels, (k + 1) * tile_pixels)
+            part = block_refs[0][place, rows, :]
+            for other in range(1, len(block_refs)):
+                part = jnp.where(scan == other, block_refs[other][place, rows, :], part)
+            top = jnp.max(jnp.abs(part), axis=0, keepdims=True)
+            level = jnp.ceil(jnp.log2(jnp.maximum(top, 1e-30) / LIMIT) * STEPS)
+            coded = jnp.round(part * jnp.exp2(level * (-1.0 / STEPS))).astype(jnp.int32)
+            slot = item * k_cols + k
+            out_ref[0, slot * tile_pixels : (slot + 1) * tile_pixels, :] = coded.astype(jnp.int16)
+            scales[slot : slot + 1, :] = level
+    out_ref[0, capacity * col_width :, :] = scales[...].astype(jnp.int32).astype(jnp.int16)
 
 
 def place_kernel(
@@ -133,10 +130,12 @@
     group = capacity * k_cols
     group_pad = -(-group // 16) * 16
 
-    point_rows = lax.all_gather(pointing, "scan", axis=1, tiled=True)
-
     small = jnp.concatenate([ground_bin, tile_lists], axis=1)
     small = lax.all_gather(small, ("tile", "scan"), axis=0, tiled=False)
+    small, pointing = lax.optimization_barrier((small, pointing))
+    point_rows = [
+        lax.all_gather(pointing[s], "scan", axis=0, tiled=True) for s in range(scan_count)
+    ]
     small = small.reshape(n_tile, n_scan, scan_count, sample_rows + k_tiles)
     ground_rows = lax.dynamic_index_in_dim(small, tile_index, 0, keepdims=False)[:, :, :sample_rows]
     ground_rows = ground_rows.transpose(1, 0, 2).reshape(scan_count, samples)
@@ -179,32 +178,51 @@
     index = found.reshape(-1).astype(jnp.int32)
 
     chunk_width = min(4 * tile_pixels, width)
+    place = scan_index[None].astype(jnp.int32)
+    blocks = []
+    for s in range(scan_count):
+        one = pl.pallas_call(
+            functools.partial(contrib_kernel, tile_pixels),
+            grid_spec=pltpu.PrefetchScalarGridSpec(
+                num_scalar_prefetch=2,
+                grid=(width // chunk_width,),
+                in_specs=[
+                    pl.BlockSpec((samples, chunk_width), lambda c, l, j: (0, c)),
+                    pl.BlockSpec((samples, col_width), lambda c, l, j: (0, j[0])),
+                    pl.BlockSpec((template_cols, samples), lambda c, l, j: (0, 0)),
+                    pl.BlockSpec((template_cols, template_cols), lambda c, l, j: (0, 0)),
+                ],
+                out_specs=pl.BlockSpec(
+                    (chunk_width // tile_pixels, col_width, tile_pixels), lambda c, l, j: (c, 0, 0)
+                ),
+                scratch_shapes=[
+                    pltpu.VMEM((col_width, samples), jnp.bfloat16),
+                    pltpu.VMEM((col_width, template_cols), jnp.float32),
+                ],
+            ),
+            out_shape=jax.ShapeDtypeStruct((k_tiles, col_width, tile_pixels), jnp.float32),
+            compiler_params=pltpu.CompilerParams(vmem_limit_bytes=58 * 1024 * 1024),
+            cost_estimate=pl.CostEstimate(
+                flops=2 * samples * width * (col_width + template_cols),
+                bytes_accessed=2 * samples * width + 4 * width * col_width,
+                transcendentals=0,
+            ),
+        )(lengths[s : s + 1], place, point_rows[s], point_rows[s], template[s], linv[s])
+        blocks.append(one)
+
+    send_rows = group * tile_pixels + group_pad
     send = pl.pallas_call(
-        functools.partial(contrib_kernel, tile_pixels, k_cols, capacity, n_tile),
+        functools.partial(code_kernel, tile_pixels, k_cols, capacity),
         grid_spec=pltpu.PrefetchScalarGridSpec(
-            num_scalar_prefetch=3,
-            grid=(scan_count, width // chunk_width),
-            in_specs=[
-                pl.BlockSpec((1, samples, chunk_width), lambda s, c, o, l, j: (s, 0, c)),
-                pl.BlockSpec((1, samples, col_width), lambda s, c, o, l, j: (s, 0, j[0])),
-                pl.BlockSpec((1, template_cols, samples), lambda s, c, o, l, j: (s, 0, 0)),
-                pl.BlockSpec((1, template_cols, template_cols), lambda s, c, o, l, j: (s, 0, 0)),
-            ],
-            out_specs=pl.BlockSpec(
-                (n_tile, group * tile_pixels + group_pad, tile_pixels), lambda s, c, o, l, j: (0, 0, 0)
-            ),
-            scratch_shapes=[
-                pltpu.VMEM((col_width, samples), jnp.bfloat16),
-                pltpu.VMEM((col_width, template_cols), jnp.float32),
-                pltpu.VMEM((row_total, col_width, tile_pixels), jnp.float32),
-                pltpu.VMEM((n_tile, group_pad, tile_pixels), jnp.float32),
-            ],
+            num_scalar_prefetch=1,
+            grid=(n_tile,),
+            in_specs=[pl.BlockSpec(b.shape, lambda d, o: (0, 0, 0)) for b in blocks],
+            out_specs=pl.BlockSpec((1, send_rows, tile_pixels), lambda d, o: (d, 0, 0)),
+            scratch_shapes=[pltpu.VMEM((group_pad, tile_pixels), jnp.float32)],
         ),
-        out_shape=jax.ShapeDtypeStruct(
-            (n_tile, group * tile_pixels + group_pad, tile_pixels), jnp.int16
-        ),
-        compiler_params=pltpu.CompilerParams(vmem_limit_bytes=48 * 1024 * 1024),
-    )(order, lengths, scan_index[None].astype(jnp.int32), point_rows, point_rows, template, linv)
+        out_shape=jax.ShapeDtypeStruct((n_tile, send_rows, tile_pixels), jnp.int16),
+        compiler_params=pltpu.CompilerParams(vmem_limit_bytes=32 * 1024 * 1024),
+    )(order, *blocks)
 
     recv = lax.all_to_all(send, "tile", split_axis=0, concat_axis=0, tiled=True)
 

time: 190 us -> 243 us (1.28)
  waiting for transfers between devices: 85.2 us -> 128 us
  local copies, waits for them, and re-layouts: 1.39 us -> 9.38 us
  Pallas kernels: 26.6 us -> 29.7 us
    all_gather x1 -> x2, waiting for transfers between devices: 36.8 us -> 79.5 us  [per_device(): lax.all_gather(pointing[s], 'scan', axis=0, tiled=True)]
    slice x0 -> x2, local copies, waits for them, and re-layouts: none -> 3.73 us  [the longest x1 3.13 us: per_device(): pointing[s]]
    pallas_call x1 -> x3, Pallas kernels: 21.4 us -> 24.5 us  [the longest x2 22.9 us: per_device(): pl.pallas_call(functools.partial(contrib_kernel, tile_pixels), grid_spec=...]
    unnamed x13 -> x15, local copies, waits for them, and re-layouts: 0.13 us -> 3.06 us
  transfers between devices with their start and end apart: 2 -> 3, of which waited for: 2 -> 3; matrix products, arithmetic and copies ran while one was open for 8% -> 7% of each run, Pallas kernels for 0% -> 5%
where the time goes in v2:
time: 243 us
  waiting for transfers between devices  128 us (53%)
  blocking collectives  43.5 us (18%)
  Pallas kernels  29.7 us (12%)
  between operations  13.6 us (6%)
  other arithmetic  13.3 us (5%)
  local copies, waits for them, and re-layouts  9.38 us (4%)
  starting transfers between devices  4.66 us (2%)
    all_gather x2, waiting for transfers between devices, per_device(): lax.all_gather(pointing[s], 'scan', axis=0, tiled=True)  79.5 us
    all_to_all x1, waiting for transfers between devices, per_device(): recv = lax.all_to_all(send, 'tile', split_axis=0, concat_axis=0, tiled=True)  47.7 us
    all_gather x1, blocking collectives, per_device(): small = lax.all_gather(small, ('tile', 'scan'), axis=0, tiled=False)  43.5 us
    pallas_call x2, Pallas kernels, per_device(): pl.pallas_call(functools.partial(contrib_kernel, tile_pixels), grid_spec=...  22.9 us
    another operation x4, other arithmetic, per_device(): factor = jnp.linalg.cholesky(normal)  6.03 us
    pallas_call x1, Pallas kernels, per_device(): pl.pallas_call(functools.partial(place_kernel, tile_pixels, group, n_tile...  5.2 us
    another operation x3, other arithmetic, per_device(): linv = jax.scipy.linalg.solve_triangular(factor, eye, lower=True)  4.99 us
  transfers between devices with their start and end apart: 3, of which 3 were waited for; matrix products, arithmetic and copies ran while one was open for 7% of the time, Pallas kernels for 5%

profile of v2, /device:TPU:0, one launch (start us, length us, event | category | flops | bytes accessed | tf_op | source)
XLA Modules:
  0.0 242.5 jit_solution(12935623316571088499)
XLA Ops:
  6.5 0.7 add_bitcast_fusion
  7.2 43.5 %all-gather.3 = s32[32,2,272]{2,1,0:T(2,128)S(1)} all-gather(s32[1,2,272]{2,1,0:T(2,128)S(1)} %add_bitcast_fusion), channel_id=2, replica_groups=mesh['scan'=8,'tile'=4] {'tile','scan'}, dimensions={0}, use_global_device_ids=true | all-gather | bytes 71808 | tf_op jit(solution)/shard_map/all_gather | solution.py:134
  50.7 3.1 %fusion.27 = (bf16[1,256,2048]{2,1,0:T(8,128)(2,1)}, bf16[1,256,2048]{2,1,0:T(8,128)(2,1)}) fusion(bf16[2,256,2048]{2,1,0:T(8,128)(2,1)} %param.6), kind=kLoop, calls=%fused_computation.96 | loop fusion | bytes 4194304 | tf_op jit(solution)/shard_map/slice | solution.py:137
  53.9 0.7 all-gather.7.cloned.1.call-update
  54.7 0.3 select_reduce_fusion
  55.2 0.4 fusion.24
  55.7 0.3 concatenate.8
  56.0 0.2 fusion.29
  56.3 5.9 %custom-call.8 = f32[2,32,32]{2,1,0:T(8,128)S(1)} custom-call(f32[2,32,32]{2,1,0:T(8,128)S(1)} %fusion.12), custom_call_target="Cholesky" | custom-call | tf_op jit(solution)/shard_map/jit(cholesky)/cholesky | solution.py:147
  62.2 0.1 compare_reduce_fusion
  62.4 4.9 %custom-call.9 = f32[2,1,32,32]{2,3,1,0:T(8,128)S(1)} custom-call(f32[2,1,32,32]{3,2,1,0:T(8,128)S(1)} %select_bitcast_fusion), custom_call_target="InvertDiagBlocksLowerTriangular" | custom-call | tf_op jit(solution)/shard_map/jit(_solve_triangular)/vmap()/triangular_solve | solution.py:149
  67.4 0.2 convert_reduce_fusion
  67.6 0.6 fusion.28
  68.2 0.1 select_reduce_fusion.3.order_ref
  68.4 0.2 fusion.9
  68.6 0.6 slice_bitcast_fusion.2
  69.2 0.7 slice_bitcast_fusion
  69.9 34.7 %all-gather.9.cloned.1.call-done = bf16[1,2048,2048]{2,1,0:T(8,128)(2,1)} async-done(((bf16[1,256,2048]{2,1,0:T(8,128)(2,1)}), bf16[1,2048,2048]{2,1,0:T(8,128)(2,1)}) %all-gather.9.cloned.1.call-update) | async-done | bytes 8388624 | tf_op jit(solution)/shard_map/all_gather | solution.py:137
  104.6 11.5 %shard_map.65.refs_1_ = f32[16,256,128]{2,1,0:T(8,128)} custom-call(s32[1]{0:T(128)} %get-tuple-element.25.lengths_ref, s32[1]{0:T(128)} %bitcast.5.place_ref, bf16[2048,2048]{1,0:T(8,128)(2,1)} %bitcast.46, bf16[2048,2048]{1,0:T(8,128)(2,1)} %bitcast.47, bf16[32,2048]{1,0:T(8,128)(2,1)} %get-tuple-element.11.template_ref, f32[32,32]{1,0:T(8,128)} %get-tuple-element.13.linv_ref), custom_call_target="tpu_custom_call" | custom-call | flops 2415919104 | bytes 10485760 | tf_op jit(solution)/shard_map/pallas_call | solution.py:184
  116.1 44.9 %all-gather.7.cloned.1.call-done = bf16[1,2048,2048]{2,1,0:T(8,128)(2,1)} async-done(((bf16[1,256,2048]{2,1,0:T(8,128)(2,1)}), bf16[1,2048,2048]{2,1,0:T(8,128)(2,1)}) %all-gather.7.cloned.1.call-update) | async-done | bytes 8388624 | tf_op jit(solution)/shard_map/all_gather | solution.py:137
  160.9 11.4 %shard_map.64.refs_0_ = f32[16,256,128]{2,1,0:T(8,128)} custom-call(s32[1]{0:T(128)} %get-tuple-element.26.lengths_ref, s32[1]{0:T(128)} %bitcast.5.place_ref, bf16[2048,2048]{1,0:T(8,128)(2,1)} %bitcast.44, bf16[2048,2048]{1,0:T(8,128)(2,1)} %bitcast.45, bf16[32,2048]{1,0:T(8,128)(2,1)} %get-tuple-element.12.template_ref, f32[32,32]{1,0:T(8,128)} %get-tuple-element.14.linv_ref), custom_call_target="tpu_custom_call" | custom-call | flops 2415919104 | bytes 10485760 | tf_op jit(solution)/shard_map/pallas_call | solution.py:184
  172.4 1.6 copy-done.2
  174.0 1.6 shard_map.66
  175.6 1.3 copy-done
  176.9 4.6 %all-to-all-start = ((s16[4,2064,128]{2,1,0:T(8,128)(2,1)}), s16[4,2064,128]{2,1,0:T(8,128)(2,1)S(1)}, u32[]{:S(2)}, u32[]{:S(2)}) async-start(s16[4,2064,128]{2,1,0:T(8,128)(2,1)} %copy-done), calls=%async_computation | async-start | bytes 4227072 | tf_op jit(solution)/shard_map/all_to_all | solution.py:227
  181.8 0.1 copy.44
  181.9 0.1 copy.41
  182.1 0.2 select_reduce_fusion.2
  182.4 0.1 copy.40
  182.6 0.1 select_n.133.index_ref
  182.8 47.7 %all-to-all-done.recv_ref = s16[4,2064,128]{2,1,0:T(8,128)(2,1)S(1)} async-done(((s16[4,2064,128]{2,1,0:T(8,128)(2,1)}), s16[4,2064,128]{2,1,0:T(8,128)(2,1)S(1)}, u32[]{:S(2)}, u32[]{:S(2)}) %all-to-all-start) | async-done | bytes 2113568 | tf_op jit(solution)/shard_map/all_to_all | solution.py:227
  230.5 5.2 %shard_map.67 = f32[1024,512]{1,0:T(8,128)} custom-call(s32[256]{0:T(256)S(1)} %select_n.133.index_ref, s16[4,2064,128]{2,1,0:T(8,128)(2,1)S(1)} %all-to-all-done.recv_ref), custom_call_target="tpu_custom_call" | custom-call | tf_op jit(solution)/shard_map/pallas_call | solution.py:229
  (49 shorter events, 1.2 us)
Async XLA Ops:
  6.5 98.1 %all-gather.9.cloned.1.call-start = ((), (), s32[]{:S(2)}) async-start(), calls=%async_computation.2 | async-start | bytes 9437184 | tf_op jit(solution)/shard_map/all_gather | solution.py:137
  53.8 0.8 copy-start.3
  53.8 0.9 copy-start.4
  53.8 1.3 copy-start.5
  53.9 107.1 %all-gather.7.cloned.1.call-start = ((), (), s32[]{:S(2)}) async-start(), calls=%async_computation.1 | async-start | bytes 9437184 | tf_op jit(solution)/shard_map/all_gather | solution.py:137
  160.9 11.4 %copy-start.1 = (f32[16,256,128]{2,1,0:T(8,128)S(1)}, f32[16,256,128]{2,1,0:T(8,128)}, u32[]{:S(2)}) copy-start(f32[16,256,128]{2,1,0:T(8,128)} %shard_map.65.refs_1_) | copy-start | bytes 6291460
  172.4 1.6 copy-start.2
  175.5 1.3 copy-start
  176.9 53.6 %all-to-all-start = ((s16[4,2064,128]{2,1,0:T(8,128)(2,1)}), s16[4,2064,128]{2,1,0:T(8,128)(2,1)S(1)}, u32[]{:S(2)}, u32[]{:S(2)}) async-start(s16[4,2064,128]{2,1,0:T(8,128)(2,1)} %copy-done), calls=%async_computation | async-start | bytes 4227072 | tf_op jit(solution)/shard_map/all_to_all | solution.py:227
Sparse Core Ops, SparseCore 0:
  54.0 50.5 all-gather.8
  106.5 54.4 all-gather.6

commit v3 on v1

--- a/solution.py
+++ b/solution.py
@@ -35,6 +35,148 @@
     return jnp.concatenate([poly_part, bins], axis=1).astype(jnp.bfloat16)
 
 
+PIECES = 4
+
+
+def gather_kernel(
+    n_scan, n_tile, point_ref, ground_ref, lists_ref, points_out, ground_out, lists_out,
+    send_sem, recv_sem, ground_send, ground_recv, lists_send, lists_recv, local_sem,
+):
+    me = lax.axis_index("scan")
+    layer = lax.axis_index("tile")
+    rows = point_ref.shape[1]
+    step = rows // PIECES
+    sibling = me + 1 - 2 * lax.rem(me, 2)
+    across_x = me + 2 - 4 * lax.rem(lax.div(me, 2), 2)
+    across_y = me + 4 - 8 * lax.rem(lax.div(me, 4), 2)
+    far = across_x + across_y - me
+
+    barrier = pltpu.get_barrier_semaphore()
+    for shift in range(1, n_scan):
+        pl.semaphore_signal(
+            barrier, inc=1, device_id={"scan": lax.rem(me + shift, n_scan)},
+            device_id_type=pl.DeviceIdType.MESH,
+        )
+    for shift in range(1, n_tile):
+        pl.semaphore_signal(
+            barrier, inc=1, device_id={"tile": lax.rem(layer + shift, n_tile)},
+            device_id_type=pl.DeviceIdType.MESH,
+        )
+    pl.semaphore_wait(barrier, n_scan + n_tile - 2)
+
+    def block(ref, owner, half, piece):
+        start = pl.multiple_of(owner * rows + piece * step, step)
+        return ref.at[half, pl.ds(start, step), :]
+
+    def send(kind, half, piece, owner, target):
+        if kind in (0, 1, 3):
+            source = point_ref.at[half, pl.ds(piece * step, step), :]
+        else:
+            source = block(points_out, owner, half, piece)
+        copy = pltpu.make_async_remote_copy(
+            src_ref=source,
+            dst_ref=block(points_out, owner, half, piece),
+            send_sem=send_sem.at[kind, half, piece],
+            recv_sem=recv_sem.at[kind, half, piece],
+            device_id={"scan": target},
+            device_id_type=pl.DeviceIdType.MESH,
+        )
+        copy.start()
+        copies[kind, half, piece] = copy
+
+    copies = {}
+    small = []
+    for piece in range(PIECES):
+        send(0, 0, piece, me, across_x)
+        send(1, 1, piece, me, across_y)
+    for shift in range(1, n_scan):
+        copy = pltpu.make_async_remote_copy(
+            src_ref=ground_ref, dst_ref=ground_out.at[me],
+            send_sem=ground_send.at[shift], recv_sem=ground_recv.at[shift],
+            device_id={"scan": lax.rem(me + shift, n_scan)},
+            device_id_type=pl.DeviceIdType.MESH,
+        )
+        copy.start()
+        small.append(copy)
+    for shift in range(1, n_tile):
+        copy = pltpu.make_async_remote_copy(
+            src_ref=lists_ref, dst_ref=lists_out.at[layer],
+            send_sem=lists_send.at[shift], recv_sem=lists_recv.at[shift],
+            device_id={"tile": lax.rem(layer + shift, n_tile)},
+            device_id_type=pl.DeviceIdType.MESH,
+        )
+        copy.start()
+        small.append(copy)
+    for piece in range(PIECES):
+        send(0, 1, piece, me, across_x)
+        send(1, 0, piece, me, across_y)
+    for half in range(2):
+        for piece in range(PIECES):
+            send(3, half, piece, me, sibling)
+    own = [
+        pltpu.make_async_copy(
+            point_ref, points_out.at[:, pl.ds(pl.multiple_of(me * rows, rows), rows), :], local_sem.at[0]
+        ),
+        pltpu.make_async_copy(ground_ref, ground_out.at[me], local_sem.at[1]),
+        pltpu.make_async_copy(lists_ref, lists_out.at[layer], local_sem.at[2]),
+    ]
+    for copy in own:
+        copy.start()
+
+    for piece in range(PIECES):
+        copies[0, 0, piece].wait_recv()
+        send(2, 0, piece, across_x, across_y)
+        copies[1, 1, piece].wait_recv()
+        send(2, 1, piece, across_y, across_x)
+        send(4, 0, piece, across_x, sibling)
+        send(5, 1, piece, across_y, sibling)
+    for piece in range(PIECES):
+        copies[0, 1, piece].wait_recv()
+        send(4, 1, piece, across_x, sibling)
+        copies[1, 0, piece].wait_recv()
+        send(5, 0, piece, across_y, sibling)
+    for piece in range(PIECES):
+        for half in range(2):
+            copies[2, half, piece].wait_recv()
+            send(6, half, piece, far, sibling)
+    for kind in range(7):
+        for half in range(2):
+            for piece in range(PIECES):
+                copies[kind, half, piece].wait_send()
+                if kind >= 3:
+                    copies[kind, half, piece].wait_recv()
+    for copy in small:
+        copy.wait()
+    for copy in own:
+        copy.wait()
+
+
+def gather_plane(pointing, ground_bin, tile_lists, n_scan, n_tile):
+    scan_count, rows, width = pointing.shape
+    anywhere = pl.BlockSpec(memory_space=pl.ANY)
+    semaphores = pltpu.SemaphoreType.DMA
+    return pl.pallas_call(
+        functools.partial(gather_kernel, n_scan, n_tile),
+        in_specs=[anywhere] * 3,
+        out_specs=[anywhere] * 3,
+        out_shape=[
+            jax.ShapeDtypeStruct((scan_count, rows * n_scan, width), pointing.dtype),
+            jax.ShapeDtypeStruct((n_scan,) + ground_bin.shape, ground_bin.dtype),
+            jax.ShapeDtypeStruct((n_tile,) + tile_lists.shape, tile_lists.dtype),
+        ],
+        scratch_shapes=[
+            semaphores((7, 2, PIECES)),
+            semaphores((7, 2, PIECES)),
+            semaphores((n_scan,)),
+            semaphores((n_scan,)),
+            semaphores((n_tile,)),
+            semaphores((n_tile,)),
+            semaphores((3,)),
+        ],
+        compiler_params=pltpu.CompilerParams(collective_id=0, has_side_effects=True),
+    )(pointing, ground_bin, tile_lists)
+
+
 def contrib_kernel(
     tile_pixels, k_cols, capacity, n_tile,
     order_ref, lengths_ref, place_ref,
@@ -133,14 +275,15 @@
     group = capacity * k_cols
     group_pad = -(-group // 16) * 16
 
-    point_rows = lax.all_gather(pointing, "scan", axis=1, tiled=True)
-
-    small = jnp.concatenate([ground_bin, tile_lists], axis=1)
-    small = lax.all_gather(small, ("tile", "scan"), axis=0, tiled=False)
-    small = small.reshape(n_tile, n_scan, scan_count, sample_rows + k_tiles)
-    ground_rows = lax.dynamic_index_in_dim(small, tile_index, 0, keepdims=False)[:, :, :sample_rows]
+    if n_scan == 8 and scan_count == 2:
+        point_rows, ground_rows, all_lists = gather_plane(
+            pointing, ground_bin, tile_lists, n_scan, n_tile
+        )
+    else:
+        point_rows = lax.all_gather(pointing, "scan", axis=1, tiled=True)
+        ground_rows = lax.all_gather(ground_bin, "scan", axis=0, tiled=False)
+        all_lists = lax.all_gather(tile_lists, "tile", axis=0, tiled=False)
     ground_rows = ground_rows.transpose(1, 0, 2).reshape(scan_count, samples)
-    all_lists = small[:, 0, :, sample_rows:]
 
     template = build_templates_t(ground_rows, lengths, degrees)
     normal = jnp.einsum("stn,sun->stu", template, template, preferred_element_type=jnp.float32)

time: 190 us -> 174 us (0.916)
  Pallas kernels: 26.6 us -> 105 us
  blocking collectives: 44.1 us -> 0 us
  waiting for transfers between devices: 85.2 us -> 48.1 us
  between operations: 13.6 us -> 0.17 us
  other arithmetic: 13.3 us -> 15.4 us
    pallas_call x0 -> x1, Pallas kernels: none -> 78.1 us  [gather_plane(): pl.pallas_call(functools.partial(gather_kernel, n_scan, n_tile), in_specs...]
    all_gather x1 -> x0, blocking collectives: 44.1 us -> none  [per_device(): small = lax.all_gather(small, ('tile', 'scan'), axis=0, tiled=False)]
    all_gather x1 -> x0, waiting for transfers between devices: 36.8 us -> none  [per_device(): point_rows = lax.all_gather(pointing, 'scan', axis=1, tiled=True)]
  transfers between devices with their start and end apart: 2 -> 1, of which waited for: 2 -> 1; matrix products, arithmetic and copies ran while one was open for 8% -> 1% of each run, Pallas kernels for 0% -> 0%
where the time goes in v3:
time: 174 us
  Pallas kernels  105 us (60%)
  waiting for transfers between devices  48.1 us (28%)
  other arithmetic  15.4 us (9%)
  starting transfers between devices  3.74 us (2%)
    pallas_call x1, Pallas kernels, gather_plane(): pl.pallas_call(functools.partial(gather_kernel, n_scan, n_tile), in_specs...  78.1 us
    all_to_all x1, waiting for transfers between devices, per_device(): recv = lax.all_to_all(send, 'tile', split_axis=0, concat_axis=0, tiled=True)  48.1 us
    pallas_call x1, Pallas kernels, per_device(): pl.pallas_call(functools.partial(contrib_kernel, tile_pixels, k_cols, cap...  21.4 us
    another operation x4, other arithmetic, per_device(): factor = jnp.linalg.cholesky(normal)  6.03 us
    pallas_call x1, Pallas kernels, per_device(): pl.pallas_call(functools.partial(place_kernel, tile_pixels, group, n_tile...  5.2 us
    another operation x3, other arithmetic, per_device(): linv = jax.scipy.linalg.solve_triangular(factor, eye, lower=True)  5 us
    all_to_all x1, starting transfers between devices, per_device(): recv = lax.all_to_all(send, 'tile', split_axis=0, concat_axis=0, tiled=True)  3.74 us
  transfers between devices with their start and end apart: 1, of which 1 were waited for; matrix products, arithmetic and copies ran while one was open for 1% of the time, Pallas kernels for 0%

profile of v3, /device:TPU:0, one launch (start us, length us, event | category | flops | bytes accessed | tf_op | source)
XLA Modules:
  0.0 173.8 jit_solution(14769465829077245191)
XLA Ops:
  0.1 0.7 convert_element_type.39
  0.7 0.7 broadcast_compare_fusion.3
  1.4 78.1 %shard_map.64 = (bf16[2,2048,2048]{2,1,0:T(8,128)(2,1)}, s32[8,2,256]{2,1,0:T(2,128)}, s32[4,2,16]{2,1,0:T(2,128)}) custom-call(bf16[2,256,2048]{2,1,0:T(8,128)(2,1)} %point_ref.1, s32[2,256]{1,0:T(2,128)} %ground_ref.1, s32[2,16]{1,0:T(2,128)} %lists_ref.1), custom_call_target="tpu_custom_call" | custom-call | tf_op jit(solution)/shard_map/pallas_call | solution.py:158
  79.5 1.0 select_reduce_fusion
  80.5 0.1 eq.106
  80.6 0.2 convert_reduce_fusion
  80.8 0.1 select_reduce_fusion.3.order_ref
  80.9 0.1 broadcast_compare_fusion
  81.0 0.8 convert_convert_fusion
  81.8 0.4 fusion.24
  82.2 0.3 concatenate.4.template_ref
  82.5 0.2 fusion.26
  82.7 0.1 copy.26
  82.8 5.9 %custom-call.8 = f32[2,32,32]{2,1,0:T(8,128)S(1)} custom-call(f32[2,32,32]{2,1,0:T(8,128)S(1)} %fusion.12), custom_call_target="Cholesky" | custom-call | tf_op jit(solution)/shard_map/jit(cholesky)/cholesky | solution.py:291
  88.7 0.1 compare_reduce_fusion
  88.8 0.1 select_bitcast_fusion
  88.9 4.9 %custom-call.9 = f32[2,1,32,32]{2,3,1,0:T(8,128)S(1)} custom-call(f32[2,1,32,32]{3,2,1,0:T(8,128)S(1)} %select_bitcast_fusion), custom_call_target="InvertDiagBlocksLowerTriangular" | custom-call | tf_op jit(solution)/shard_map/jit(_solve_triangular)/vmap()/triangular_solve | solution.py:293
  93.8 0.3 fusion.9.linv_ref
  94.1 21.4 %shard_map.65 = s16[4,2064,128]{2,1,0:T(8,128)(2,1)} custom-call(s32[32]{0:T(128)S(1)} %select_reduce_fusion.3.order_ref, s32[2]{0:T(128)S(1)} %copy-done, s32[1]{0:T(128)} %bitcast.1.place_ref, bf16[2,2048,2048]{2,1,0:T(8,128)(2,1)} %get-tuple-element.9.point_ref.own_ref, bf16[2,2048,2048]{2,1,0:T(8,128)(2,1)} %get-tuple-element.9.point_ref.own_ref, ...), custom_call_target="tpu_custom_call" | custom-call | tf_op jit(solution)/shard_map/pallas_call | solution.py:325
  115.5 3.7 %all-to-all-start = ((s16[4,2064,128]{2,1,0:T(8,128)(2,1)}), s16[4,2064,128]{2,1,0:T(8,128)(2,1)S(1)}, u32[]{:S(2)}, u32[]{:S(2)}) async-start(s16[4,2064,128]{2,1,0:T(8,128)(2,1)} %shard_map.65), calls=%async_computation | async-start | bytes 4227072 | tf_op jit(solution)/shard_map/all_to_all | solution.py:352
  119.2 0.1 dynamic-slice_subtract_fusion
  119.3 0.1 copy.21
  119.4 0.1 select_reduce_fusion.4
  119.5 0.1 copy.25
  119.6 0.1 copy.22
  119.7 0.1 add.157
  119.8 0.2 select_reduce_fusion.2
  120.1 0.1 copy.19
  120.2 0.1 copy.24
  120.3 0.1 select_n.127.index_ref
  120.5 48.1 %all-to-all-done.recv_ref = s16[4,2064,128]{2,1,0:T(8,128)(2,1)S(1)} async-done(((s16[4,2064,128]{2,1,0:T(8,128)(2,1)}), s16[4,2064,128]{2,1,0:T(8,128)(2,1)S(1)}, u32[]{:S(2)}, u32[]{:S(2)}) %all-to-all-start) | async-done | bytes 2113568 | tf_op jit(solution)/shard_map/all_to_all | solution.py:352
  168.6 5.2 %shard_map.66 = f32[1024,512]{1,0:T(8,128)} custom-call(s32[256]{0:T(256)S(1)} %select_n.127.index_ref, s16[4,2064,128]{2,1,0:T(8,128)(2,1)S(1)} %all-to-all-done.recv_ref), custom_call_target="tpu_custom_call" | custom-call | tf_op jit(solution)/shard_map/pallas_call | solution.py:354
  (23 shorter events, 0.2 us)
Async XLA Ops:
  0.0 94.1 %copy-start = (s32[2]{0:T(128)S(1)}, s32[2]{0:T(128)}, u32[]{:S(2)}) copy-start(s32[2]{0:T(128)} %lengths_ref.1) | copy-start | bytes 28
  0.0 79.5 %copy-start.2 = (s32[32]{0:T(128)S(1)}, s32[32]{0:T(128)}, u32[]{:S(2)}) copy-start(s32[32]{0:T(128)} %param.11) | copy-start | bytes 388
  115.5 3.8 %copy-start.1 = (s32[4,2,16]{2,1,0:T(2,128)S(1)}, s32[4,2,16]{2,1,0:T(2,128)}, u32[]{:S(2)}) copy-start(s32[4,2,16]{2,1,0:T(2,128)} %get-tuple-element.8) | copy-start | bytes 1540
  115.5 53.2 %all-to-all-start = ((s16[4,2064,128]{2,1,0:T(8,128)(2,1)}), s16[4,2064,128]{2,1,0:T(8,128)(2,1)S(1)}, u32[]{:S(2)}, u32[]{:S(2)}) async-start(s16[4,2064,128]{2,1,0:T(8,128)(2,1)} %shard_map.65), calls=%async_computation | async-start | bytes 4227072 | tf_op jit(solution)/shard_map/all_to_all | solution.py:352

commit v4 on v3

--- a/solution.py
+++ b/solution.py
@@ -35,7 +35,7 @@
     return jnp.concatenate([poly_part, bins], axis=1).astype(jnp.bfloat16)
 
 
-PIECES = 4
+PIECES = 8
 
 
 def gather_kernel(

time: 174 us -> 175 us (level)
  no operation moved by 1% of the time
where the time goes in v4:
time: 175 us; the launch traced here: 174 us
  Pallas kernels  105 us (60%)
  waiting for transfers between devices  48.1 us (27%)
  other arithmetic  15.4 us (9%)
  starting transfers between devices  3.74 us (2%)
    pallas_call x1, Pallas kernels, gather_plane(): pl.pallas_call(functools.partial(gather_kernel, n_scan, n_tile), in_specs...  78.7 us
    all_to_all x1, waiting for transfers between devices, per_device(): recv = lax.all_to_all(send, 'tile', split_axis=0, concat_axis=0, tiled=True)  48.1 us
    pallas_call x1, Pallas kernels, per_device(): pl.pallas_call(functools.partial(contrib_kernel, tile_pixels, k_cols, cap...  21.4 us
    another operation x4, other arithmetic, per_device(): factor = jnp.linalg.cholesky(normal)  6.03 us
    pallas_call x1, Pallas kernels, per_device(): pl.pallas_call(functools.partial(place_kernel, tile_pixels, group, n_tile...  5.2 us
    another operation x3, other arithmetic, per_device(): linv = jax.scipy.linalg.solve_triangular(factor, eye, lower=True)  5 us
    all_to_all x1, starting transfers between devices, per_device(): recv = lax.all_to_all(send, 'tile', split_axis=0, concat_axis=0, tiled=True)  3.74 us
  transfers between devices with their start and end apart: 1, of which 1 were waited for; matrix products, arithmetic and copies ran while one was open for 1% of the time, Pallas kernels for 0%

profile of v4, /device:TPU:0, one launch (start us, length us, event | category | flops | bytes accessed | tf_op | source)
XLA Modules:
  0.0 174.5 jit_solution(10030874339656748482)
XLA Ops:
  0.1 0.7 convert_element_type.39
  0.7 0.7 broadcast_compare_fusion.3
  1.4 78.7 %shard_map.64 = (bf16[2,2048,2048]{2,1,0:T(8,128)(2,1)}, s32[8,2,256]{2,1,0:T(2,128)}, s32[4,2,16]{2,1,0:T(2,128)}) custom-call(bf16[2,256,2048]{2,1,0:T(8,128)(2,1)} %point_ref.1, s32[2,256]{1,0:T(2,128)} %ground_ref.1, s32[2,16]{1,0:T(2,128)} %lists_ref.1), custom_call_target="tpu_custom_call" | custom-call | tf_op jit(solution)/shard_map/pallas_call | solution.py:158
  80.1 1.0 select_reduce_fusion
  81.1 0.1 eq.106
  81.2 0.2 convert_reduce_fusion
  81.5 0.1 select_reduce_fusion.3.order_ref
  81.6 0.1 broadcast_compare_fusion
  81.7 0.8 convert_convert_fusion
  82.4 0.4 fusion.24
  82.8 0.3 concatenate.4.template_ref
  83.1 0.2 fusion.26
  83.3 0.1 copy.26
  83.4 5.9 %custom-call.8 = f32[2,32,32]{2,1,0:T(8,128)S(1)} custom-call(f32[2,32,32]{2,1,0:T(8,128)S(1)} %fusion.12), custom_call_target="Cholesky" | custom-call | tf_op jit(solution)/shard_map/jit(cholesky)/cholesky | solution.py:291
  89.3 0.1 compare_reduce_fusion
  89.5 0.1 select_bitcast_fusion
  89.5 4.9 %custom-call.9 = f32[2,1,32,32]{2,3,1,0:T(8,128)S(1)} custom-call(f32[2,1,32,32]{3,2,1,0:T(8,128)S(1)} %select_bitcast_fusion), custom_call_target="InvertDiagBlocksLowerTriangular" | custom-call | tf_op jit(solution)/shard_map/jit(_solve_triangular)/vmap()/triangular_solve | solution.py:293
  94.4 0.3 fusion.9.linv_ref
  94.7 21.4 %shard_map.65 = s16[4,2064,128]{2,1,0:T(8,128)(2,1)} custom-call(s32[32]{0:T(128)S(1)} %select_reduce_fusion.3.order_ref, s32[2]{0:T(128)S(1)} %copy-done, s32[1]{0:T(128)} %bitcast.1.place_ref, bf16[2,2048,2048]{2,1,0:T(8,128)(2,1)} %get-tuple-element.9.point_ref.own_ref, bf16[2,2048,2048]{2,1,0:T(8,128)(2,1)} %get-tuple-element.9.point_ref.own_ref, ...), custom_call_target="tpu_custom_call" | custom-call | tf_op jit(solution)/shard_map/pallas_call | solution.py:325
  116.1 3.7 %all-to-all-start = ((s16[4,2064,128]{2,1,0:T(8,128)(2,1)}), s16[4,2064,128]{2,1,0:T(8,128)(2,1)S(1)}, u32[]{:S(2)}, u32[]{:S(2)}) async-start(s16[4,2064,128]{2,1,0:T(8,128)(2,1)} %shard_map.65), calls=%async_computation | async-start | bytes 4227072 | tf_op jit(solution)/shard_map/all_to_all | solution.py:352
  119.9 0.1 dynamic-slice_subtract_fusion
  119.9 0.1 copy.21
  120.0 0.1 select_reduce_fusion.4
  120.1 0.1 copy.25
  120.2 0.1 copy.22
  120.4 0.1 add.157
  120.5 0.2 select_reduce_fusion.2
  120.7 0.1 copy.19
  120.8 0.1 copy.24
  121.0 0.1 select_n.127.index_ref
  121.1 48.1 %all-to-all-done.recv_ref = s16[4,2064,128]{2,1,0:T(8,128)(2,1)S(1)} async-done(((s16[4,2064,128]{2,1,0:T(8,128)(2,1)}), s16[4,2064,128]{2,1,0:T(8,128)(2,1)S(1)}, u32[]{:S(2)}, u32[]{:S(2)}) %all-to-all-start) | async-done | bytes 2113568 | tf_op jit(solution)/shard_map/all_to_all | solution.py:352
  169.3 5.2 %shard_map.66 = f32[1024,512]{1,0:T(8,128)} custom-call(s32[256]{0:T(256)S(1)} %select_n.127.index_ref, s16[4,2064,128]{2,1,0:T(8,128)(2,1)S(1)} %all-to-all-done.recv_ref), custom_call_target="tpu_custom_call" | custom-call | tf_op jit(solution)/shard_map/pallas_call | solution.py:354
  (23 shorter events, 0.2 us)
Async XLA Ops:
  0.0 94.7 %copy-start = (s32[2]{0:T(128)S(1)}, s32[2]{0:T(128)}, u32[]{:S(2)}) copy-start(s32[2]{0:T(128)} %lengths_ref.1) | copy-start | bytes 28
  0.0 80.1 %copy-start.2 = (s32[32]{0:T(128)S(1)}, s32[32]{0:T(128)}, u32[]{:S(2)}) copy-start(s32[32]{0:T(128)} %param.11) | copy-start | bytes 388
  116.1 3.8 %copy-start.1 = (s32[4,2,16]{2,1,0:T(2,128)S(1)}, s32[4,2,16]{2,1,0:T(2,128)}, u32[]{:S(2)}) copy-start(s32[4,2,16]{2,1,0:T(2,128)} %get-tuple-element.8) | copy-start | bytes 1540
  116.1 53.2 %all-to-all-start = ((s16[4,2064,128]{2,1,0:T(8,128)(2,1)}), s16[4,2064,128]{2,1,0:T(8,128)(2,1)S(1)}, u32[]{:S(2)}, u32[]{:S(2)}) async-start(s16[4,2064,128]{2,1,0:T(8,128)(2,1)} %shard_map.65), calls=%async_computation | async-start | bytes 4227072 | tf_op jit(solution)/shard_map/all_to_all | solution.py:352

commit v5 on v3

--- a/solution.py
+++ b/solution.py
@@ -321,7 +321,7 @@
     )
     index = found.reshape(-1).astype(jnp.int32)
 
-    chunk_width = min(4 * tile_pixels, width)
+    chunk_width = min(8 * tile_pixels, width)
     send = pl.pallas_call(
         functools.partial(contrib_kernel, tile_pixels, k_cols, capacity, n_tile),
         grid_spec=pltpu.PrefetchScalarGridSpec(

time: 174 us -> 172 us (0.989)
  Pallas kernels: 105 us -> 103 us
    pallas_call x1, Pallas kernels: 21.4 us -> 19.4 us  [per_device(): pl.pallas_call(functools.partial(contrib_kernel, tile_pixels, k_cols, cap...]
where the time goes in v5:
time: 172 us
  Pallas kernels  103 us (60%)
  waiting for transfers between devices  48 us (28%)
  other arithmetic  15.4 us (9%)
  starting transfers between devices  3.74 us (2%)
    pallas_call x1, Pallas kernels, gather_plane(): pl.pallas_call(functools.partial(gather_kernel, n_scan, n_tile), in_specs...  78.1 us
    all_to_all x1, waiting for transfers between devices, per_device(): recv = lax.all_to_all(send, 'tile', split_axis=0, concat_axis=0, tiled=True)  48 us
    pallas_call x1, Pallas kernels, per_device(): pl.pallas_call(functools.partial(contrib_kernel, tile_pixels, k_cols, cap...  19.4 us
    another operation x4, other arithmetic, per_device(): factor = jnp.linalg.cholesky(normal)  6.03 us
    pallas_call x1, Pallas kernels, per_device(): pl.pallas_call(functools.partial(place_kernel, tile_pixels, group, n_tile...  5.2 us
    another operation x3, other arithmetic, per_device(): linv = jax.scipy.linalg.solve_triangular(factor, eye, lower=True)  5 us
    all_to_all x1, starting transfers between devices, per_device(): recv = lax.all_to_all(send, 'tile', split_axis=0, concat_axis=0, tiled=True)  3.74 us
  transfers between devices with their start and end apart: 1, of which 1 were waited for; matrix products, arithmetic and copies ran while one was open for 1% of the time, Pallas kernels for 0%

profile of v5, /device:TPU:0, one launch (start us, length us, event | category | flops | bytes accessed | tf_op | source)
XLA Modules:
  0.0 171.7 jit_solution(9491568348280520173)
XLA Ops:
  0.1 0.7 convert_element_type.39
  0.7 0.7 broadcast_compare_fusion.3
  1.4 78.1 %shard_map.64 = (bf16[2,2048,2048]{2,1,0:T(8,128)(2,1)}, s32[8,2,256]{2,1,0:T(2,128)}, s32[4,2,16]{2,1,0:T(2,128)}) custom-call(bf16[2,256,2048]{2,1,0:T(8,128)(2,1)} %point_ref.1, s32[2,256]{1,0:T(2,128)} %ground_ref.1, s32[2,16]{1,0:T(2,128)} %lists_ref.1), custom_call_target="tpu_custom_call" | custom-call | tf_op jit(solution)/shard_map/pallas_call | solution.py:158
  79.5 1.0 select_reduce_fusion
  80.5 0.1 eq.106
  80.6 0.2 convert_reduce_fusion
  80.8 0.1 select_reduce_fusion.3.order_ref
  80.9 0.1 broadcast_compare_fusion
  81.0 0.8 convert_convert_fusion
  81.8 0.4 fusion.24
  82.2 0.3 concatenate.4.template_ref
  82.5 0.2 fusion.26
  82.7 0.1 copy.26
  82.8 5.9 %custom-call.8 = f32[2,32,32]{2,1,0:T(8,128)S(1)} custom-call(f32[2,32,32]{2,1,0:T(8,128)S(1)} %fusion.12), custom_call_target="Cholesky" | custom-call | tf_op jit(solution)/shard_map/jit(cholesky)/cholesky | solution.py:291
  88.7 0.1 compare_reduce_fusion
  88.8 0.1 select_bitcast_fusion
  88.9 4.9 %custom-call.9 = f32[2,1,32,32]{2,3,1,0:T(8,128)S(1)} custom-call(f32[2,1,32,32]{3,2,1,0:T(8,128)S(1)} %select_bitcast_fusion), custom_call_target="InvertDiagBlocksLowerTriangular" | custom-call | tf_op jit(solution)/shard_map/jit(_solve_triangular)/vmap()/triangular_solve | solution.py:293
  93.8 0.3 fusion.9.linv_ref
  94.1 19.4 %shard_map.65 = s16[4,2064,128]{2,1,0:T(8,128)(2,1)} custom-call(s32[32]{0:T(128)S(1)} %select_reduce_fusion.3.order_ref, s32[2]{0:T(128)S(1)} %copy-done, s32[1]{0:T(128)} %bitcast.1.place_ref, bf16[2,2048,2048]{2,1,0:T(8,128)(2,1)} %get-tuple-element.9.point_ref.own_ref, bf16[2,2048,2048]{2,1,0:T(8,128)(2,1)} %get-tuple-element.9.point_ref.own_ref, ...), custom_call_target="tpu_custom_call" | custom-call | tf_op jit(solution)/shard_map/pallas_call | solution.py:325
  113.5 3.7 %all-to-all-start = ((s16[4,2064,128]{2,1,0:T(8,128)(2,1)}), s16[4,2064,128]{2,1,0:T(8,128)(2,1)S(1)}, u32[]{:S(2)}, u32[]{:S(2)}) async-start(s16[4,2064,128]{2,1,0:T(8,128)(2,1)} %shard_map.65), calls=%async_computation | async-start | bytes 4227072 | tf_op jit(solution)/shard_map/all_to_all | solution.py:352
  117.2 0.1 dynamic-slice_subtract_fusion
  117.3 0.1 copy.21
  117.4 0.1 select_reduce_fusion.4
  117.5 0.1 copy.25
  117.6 0.1 copy.22
  117.8 0.1 add.157
  117.9 0.2 select_reduce_fusion.2
  118.1 0.1 copy.19
  118.2 0.1 copy.24
  118.4 0.1 select_n.127.index_ref
  118.5 48.0 %all-to-all-done.recv_ref = s16[4,2064,128]{2,1,0:T(8,128)(2,1)S(1)} async-done(((s16[4,2064,128]{2,1,0:T(8,128)(2,1)}), s16[4,2064,128]{2,1,0:T(8,128)(2,1)S(1)}, u32[]{:S(2)}, u32[]{:S(2)}) %all-to-all-start) | async-done | bytes 2113568 | tf_op jit(solution)/shard_map/all_to_all | solution.py:352
  166.5 5.2 %shard_map.66 = f32[1024,512]{1,0:T(8,128)} custom-call(s32[256]{0:T(256)S(1)} %select_n.127.index_ref, s16[4,2064,128]{2,1,0:T(8,128)(2,1)S(1)} %all-to-all-done.recv_ref), custom_call_target="tpu_custom_call" | custom-call | tf_op jit(solution)/shard_map/pallas_call | solution.py:354
  (23 shorter events, 0.2 us)
Async XLA Ops:
  0.0 94.1 %copy-start = (s32[2]{0:T(128)S(1)}, s32[2]{0:T(128)}, u32[]{:S(2)}) copy-start(s32[2]{0:T(128)} %lengths_ref.1) | copy-start | bytes 28
  0.0 79.5 %copy-start.2 = (s32[32]{0:T(128)S(1)}, s32[32]{0:T(128)}, u32[]{:S(2)}) copy-start(s32[32]{0:T(128)} %param.11) | copy-start | bytes 388
  113.5 3.8 %copy-start.1 = (s32[4,2,16]{2,1,0:T(2,128)S(1)}, s32[4,2,16]{2,1,0:T(2,128)}, u32[]{:S(2)}) copy-start(s32[4,2,16]{2,1,0:T(2,128)} %get-tuple-element.8) | copy-start | bytes 1540
  113.5 53.1 %all-to-all-start = ((s16[4,2064,128]{2,1,0:T(8,128)(2,1)}), s16[4,2064,128]{2,1,0:T(8,128)(2,1)S(1)}, u32[]{:S(2)}, u32[]{:S(2)}) async-start(s16[4,2064,128]{2,1,0:T(8,128)(2,1)} %shard_map.65), calls=%async_computation | async-start | bytes 4227072 | tf_op jit(solution)/shard_map/all_to_all | solution.py:352
